TPU v7x, 32 devices: a whole 2x2x4 slice. The times are simulated.
32 devices in a mesh: tm: 4 (over z), height: 8 (over y, x, core).
Axes of the slice: x: 2, y: 2, z: 4, core: 2. Of those that a mesh axis runs over, the one named last changes fastest.
Arguments:
- latents: bfloat16 [9, 16, 128, 384], P(None, 'height', 'tm'), may hold values from -6 to 6
- gain_in: float32 [384], replicated, may hold values from 0.1 to 1.9
- weight_in: bfloat16 [3, 3, 3, 384, 384], replicated, may hold values from -0.0625 to 0.0625
- bias_in: float32 [384], replicated, may hold values from -3 to 3
- gain_mid: float32 [384], replicated, may hold values from 0.1 to 1.9
- weight_mid: bfloat16 [3, 3, 3, 384, 384], replicated, may hold values from -0.0625 to 0.0625
- bias_mid: float32 [384], replicated, may hold values from -2 to 2
- up_weight: bfloat16 [3, 3, 384, 192], replicated, may hold values from -0.109375 to 0.109375
- up_bias: float32 [192], replicated, may hold values from -2 to 2
Outputs:
- first_image: bfloat16 [32, 256, 192], P('height', 'tm')
- later_images: bfloat16 [8, 32, 256, 192], P('tm', 'height')
All inputs are finite; a program needn't handle non-finite values.
Results may differ from a plain program's by a relative error of at most 0.0053.
Values may be sent and summed in bfloat16 or wider, within the bound.
A program may use at most 128 MiB of HBM per device.

v0:
```python
import functools

import jax
import jax.numpy as jnp
from jax import lax
from jax.experimental import pallas as pl
from jax.experimental.pallas import tpu as pltpu
from jax.sharding import PartitionSpec as P

epsilon = 1e-06
MESH = pl.DeviceIdType.MESH
AROUND = [(-1, 0), (1, 0), (0, -1), (0, 1), (-1, -1), (-1, 1), (1, -1), (1, 1)]


def rounded_up(count):
    return -(-count // 16) * 16


def normed_silu(values, norm_gain):
    factor = lax.rsqrt(jnp.mean(values * values, axis=-1, keepdims=True) + epsilon)
    scaled = values * factor * norm_gain
    return scaled / (1.0 + jnp.exp(-scaled))


def present(dh, dt, h, t, sizes):
    ok = (h + dh >= 0) & (h + dh < sizes[0])
    return ok & (t + dt >= 0) & (t + dt < sizes[1])


def spans_of(frames, rows, cols):
    lengths = [frames * cols] * 2 + [frames * rows] * 2 + [frames] * 4
    spans, start = [], 0
    for length in lengths:
        spans.append((start, length))
        start += rounded_up(length)
    return spans, start


def rim_pack(values):
    channels = values.shape[-1]
    pieces = []
    for dh, dt in AROUND:
        piece = values
        if dh:
            piece = piece[:, :1] if dh < 0 else piece[:, -1:]
        if dt:
            piece = piece[:, :, :1] if dt < 0 else piece[:, :, -1:]
        piece = piece.reshape(-1, channels)
        pieces.append(jnp.pad(piece, ((0, rounded_up(piece.shape[0]) - piece.shape[0]), (0, 0))))
    return jnp.concatenate(pieces, axis=0)


def rim_kernel(spans, sizes, src, dst, send_sems, recv_sems):
    h, t = lax.axis_index("height"), lax.axis_index("tm")
    barrier = pltpu.get_barrier_semaphore()
    there = [present(dh, dt, h, t, sizes) for dh, dt in AROUND]
    for ok, (dh, dt) in zip(there, AROUND):

        @pl.when(ok)
        def _():
            pl.semaphore_signal(barrier, inc=1, device_id=(t + dt, h + dh), device_id_type=MESH)

    pl.semaphore_wait(barrier, sum(ok.astype(jnp.int32) for ok in there))

    def copy(k):
        dh, dt = AROUND[k]
        start, length = spans[k]
        part = pl.ds(start, rounded_up(length))
        return pltpu.make_async_remote_copy(
            src_ref=src.at[part],
            dst_ref=dst.at[part],
            send_sem=send_sems.at[k],
            recv_sem=recv_sems.at[k],
            device_id=(t + dt, h + dh),
            device_id_type=MESH,
        )

    for k in range(8):

        @pl.when(there[k])
        def _():
            copy(k).start()

    for k in range(8):

        @pl.when(there[k])
        def _():
            copy(k).wait_send()

    for k in range(8):
        dh, dt = AROUND[k]

        @pl.when(present(-dh, -dt, h, t, sizes))
        def _():
            copy(k).wait_recv()


def exchanged(values, collective_id):
    frames, rows, cols, channels = values.shape
    spans, total = spans_of(frames, rows, cols)
    sizes = lax.axis_size("height"), lax.axis_size("tm")
    return pl.pallas_call(
        functools.partial(rim_kernel, spans, sizes),
        out_shape=jax.ShapeDtypeStruct((total, channels), values.dtype),
        in_specs=[pl.BlockSpec(memory_space=pl.ANY)],
        out_specs=pl.BlockSpec(memory_space=pl.ANY),
        scratch_shapes=[pltpu.SemaphoreType.DMA((8,)), pltpu.SemaphoreType.DMA((8,))],
        compiler_params=pltpu.CompilerParams(collective_id=collective_id, has_side_effects=True),
    )(rim_pack(values))


def spread_kernel(spans, line, sizes, first, later, first_out, later_out, edge_out, fs, fr, ls, lr, es, er, own_sem):
    h, t = lax.axis_index("height"), lax.axis_index("tm")
    tops, groups = sizes
    barrier = pltpu.get_barrier_semaphore()
    eight = [present(*way, h, t, sizes) for way in AROUND]
    ups = h >= 1, h + 1 < tops

    def to(j):
        return (lax.rem(t + j, groups), h)

    for j in range(1, groups):
        pl.semaphore_signal(barrier, inc=1, device_id=to(j), device_id_type=MESH)
    for k, (dh, dt) in enumerate(AROUND):
        if dh:

            @pl.when(eight[k])
            def _(dh=dh, dt=dt):
                pl.semaphore_signal(
                    barrier, inc=1, device_id=(t + dt, h + dh), device_id_type=MESH
                )

    pl.semaphore_wait(
        barrier,
        groups - 1 + sum(eight[k].astype(jnp.int32) for k in range(8) if AROUND[k][0]),
    )

    def later_copy(j):
        return pltpu.make_async_remote_copy(
            src_ref=later.at[lax.rem(t + j, groups)],
            dst_ref=later_out.at[t],
            send_sem=ls.at[j],
            recv_sem=lr.at[j],
            device_id=to(j),
            device_id_type=MESH,
        )

    def first_copy(k):
        dh, dt = AROUND[k]
        part = pl.ds(spans[k][0], rounded_up(spans[k][1]))
        return pltpu.make_async_remote_copy(
            src_ref=first.at[part],
            dst_ref=first_out.at[part],
            send_sem=fs.at[k],
            recv_sem=fr.at[k],
            device_id=(t + dt, h + dh),
            device_id_type=MESH,
        )

    def edge_copy(j, side):
        owner = lax.rem(t + groups - j, groups)
        start = 0 if side == 0 else later.shape[1] - line
        source = later.at[t] if j == 0 else later_out.at[owner]
        return pltpu.make_async_remote_copy(
            src_ref=source.at[pl.ds(start, line)],
            dst_ref=edge_out.at[side, owner],
            send_sem=es.at[side, j],
            recv_sem=er.at[side, j],
            device_id=(t, h + (-1 if side == 0 else 1)),
            device_id_type=MESH,
        )

    for j in (2, 1, 3) if groups == 4 else range(1, groups):
        later_copy(j).start()
    own = pltpu.make_async_copy(later.at[t], later_out.at[t], own_sem)
    own.start()
    for k in range(8):
        pl.when(eight[k])(lambda k=k: first_copy(k).start())
    for j in range(groups):
        if j:
            later_copy(j).wait_recv()
        for side in range(2):
            pl.when(ups[side])(lambda j=j, side=side: edge_copy(j, side).start())
    own.wait()
    for j in range(1, groups):
        later_copy(j).wait_send()
    for k in range(8):
        dh, dt = AROUND[k]
        pl.when(eight[k])(lambda k=k: first_copy(k).wait_send())
        pl.when(present(-dh, -dt, h, t, sizes))(lambda k=k: first_copy(k).wait_recv())
    for j in range(groups):
        for side in range(2):
            pl.when(ups[side])(lambda j=j, side=side: edge_copy(j, side).wait_send())
            pl.when(ups[1 - side])(lambda j=j, side=side: edge_copy(j, side).wait_recv())


def spread(summed):
    frames, rows, cols, channels = summed.shape
    groups = lax.axis_size("tm")
    sizes = lax.axis_size("height"), groups
    held = (frames - 1) // groups
    spans, total = spans_of(1, rows, cols)
    line = held * cols
    later = summed[1:].reshape(groups, held, rows, cols, channels).transpose(0, 2, 1, 3, 4)
    later = later.reshape(groups, rows * line, channels)
    anywhere = pl.BlockSpec(memory_space=pl.ANY)
    dma = pltpu.SemaphoreType.DMA
    return pl.pallas_call(
        functools.partial(spread_kernel, spans, line, sizes),
        out_shape=(
            jax.ShapeDtypeStruct((total, channels), summed.dtype),
            jax.ShapeDtypeStruct(later.shape, summed.dtype),
            jax.ShapeDtypeStruct((2, groups, line, channels), summed.dtype),
        ),
        in_specs=[anywhere] * 2,
        out_specs=(anywhere,) * 3,
        scratch_shapes=[dma((8,))] * 2 + [dma((groups,))] * 2 + [dma((2, groups))] * 2 + [dma],
        compiler_params=pltpu.CompilerParams(collective_id=2, has_side_effects=True),
    )(rim_pack(summed[:1]), later)


def rim_lines(values, rim, spans, sizes, frame):
    frames, rows, cols, channels = values.shape
    h, t = lax.axis_index("height"), lax.axis_index("tm")
    lines = []
    for r in range(rows + 2):
        dh = -1 if r == 0 else 1 if r == rows + 1 else 0

        def piece(dt, start_of, length):
            k = AROUND.index((-dh, -dt))
            base = spans[k][0] + start_of // 16 * 16
            size = rounded_up(length) if length > 1 else 16
            value = rim[base : base + size].astype(jnp.float32)
            value = value[start_of % 16 : start_of % 16 + length]
            return jnp.where(present(dh, dt, h, t, sizes), value, 0.0)

        if dh:
            line = piece(0, frame * cols, cols)
            sides = [piece(dt, frame, 1) for dt in (-1, 1)]
        else:
            line = values[frame, r - 1].astype(jnp.float32)
            sides = [piece(dt, frame * rows + r - 1, 1) for dt in (-1, 1)]
        lines.append((line, sides[0], sides[1]))
    return lines


def conv_kernel(spans, sizes, residual, x, rim, w, bias, other, out, buf, acc):
    frames, rows, cols, channels = x.shape
    step = pl.program_id(0)

    @pl.when(step == 0)
    def _():
        acc[...] = jnp.broadcast_to(bias[...], acc.shape)
        buf[:, 0:2] = jnp.zeros((3, 2, *buf.shape[2:]), buf.dtype)
        place = lax.broadcasted_iota(jnp.int32, (cols, channels), 0)
        for f in range(frames):
            for r, (line, left, right) in enumerate(rim_lines(x, rim, spans, sizes, f)):
                buf[0, f + 2, r] = jnp.where(place == 0, left, pltpu.roll(line, 1, 0)).astype(buf.dtype)
                buf[1, f + 2, r] = line.astype(buf.dtype)
                buf[2, f + 2, r] = jnp.where(
                    place == cols - 1, right, pltpu.roll(line, cols - 1, 0)
                ).astype(buf.dtype)

    a, b = step // 3, step % 3
    total = acc[...]
    for c in range(3):
        cells = buf[c, pl.ds(a, frames), pl.ds(b, rows)].reshape(frames * rows * cols, channels)
        total = total + jnp.dot(cells, w[0, 0, c], preferred_element_type=jnp.float32)
    acc[...] = total

    @pl.when(step == 8)
    def _():
        if residual:
            ended = other[...].reshape(acc.shape).astype(jnp.float32) + acc[...]
        else:
            ended = normed_silu(acc[...], other[...])
        out[...] = ended.astype(out.dtype).reshape(out.shape)


def conv(values, weight, bias, other, collective_id, residual):
    frames, rows, cols, channels = values.shape
    spans, _ = spans_of(frames, rows, cols)
    sizes = lax.axis_size("height"), lax.axis_size("tm")
    rim = exchanged(values, collective_id)
    bias = bias.reshape(1, channels)
    if not residual:
        other = other.reshape(1, channels)

    def whole(array):
        return pl.BlockSpec(array.shape, lambda i: (0,) * array.ndim)

    return pl.pallas_call(
        functools.partial(conv_kernel, spans, sizes, residual),
        out_shape=jax.ShapeDtypeStruct(values.shape, values.dtype),
        grid=(9,),
        in_specs=[
            whole(values),
            whole(rim),
            pl.BlockSpec((1, 1, *weight.shape[2:]), lambda i: (i // 3, i % 3, 0, 0, 0)),
            whole(bias),
            whole(other),
        ],
        out_specs=whole(values),
        scratch_shapes=[
            pltpu.VMEM((3, frames + 2, rows + 2, cols, channels), values.dtype),
            pltpu.VMEM((frames * rows * cols, channels), jnp.float32),
        ],
        compiler_params=pltpu.CompilerParams(vmem_limit_bytes=40 * 2**20),
    )(values, rim, weight, bias, other)


def doubling(cols, offset):
    at = lax.broadcasted_iota(jnp.int32, (2 * cols, cols), 0) + (offset - 1)
    source = 2 * lax.broadcasted_iota(jnp.int32, (2 * cols, cols), 1)
    return ((at == source) | (at == source + 1)).astype(jnp.bfloat16)


def up_kernel(spans, sizes, frame0, rim, later, edge, w, bias_row, bias_col, first_out, later_out):
    _, rows, cols, channels = frame0.shape
    groups = later.shape[0]
    held = later_out.shape[0]
    line = held * cols
    h = lax.axis_index("height")
    taps = {}
    for c in range(3):
        wide = [w[b, c].astype(jnp.float32) for b in range(3)]
        taps[0, 0, c], taps[1, 1, c] = w[0, c], w[2, c]
        taps[0, 1, c] = (wide[1] + wide[2]).astype(jnp.bfloat16)
        taps[1, 0, c] = (wide[0] + wide[1]).astype(jnp.bfloat16)
    last_dims = (((1,), (1,)), ((), ()))

    def doubled(matrix, values):
        return jnp.dot(matrix, values, preferred_element_type=jnp.float32)

    spreads = [doubling(groups * cols, c) for c in range(3)]
    for f in range(held):
        wide_rows = []
        for r in range(rows + 2):
            parts = []
            for s in range(groups):
                if r == 0:
                    part = jnp.where(h >= 1, edge[1, s, f * cols : (f + 1) * cols], 0)
                elif r == rows + 1:
                    part = jnp.where(h + 1 < sizes[0], edge[0, s, f * cols : (f + 1) * cols], 0)
                else:
                    start = (r - 1) * line + f * cols
                    part = later[s, start : start + cols]
                parts.append(part)
            whole = jnp.concatenate(parts, axis=0)
            wide_rows.append([doubled(m, whole).astype(jnp.bfloat16) for m in spreads])
        for r in range(rows):
            for parity in range(2):
                total = bias_col[...]
                for step in range(2):
                    for c in range(3):
                        total = total + lax.dot_general(
                            taps[parity, step, c],
                            wide_rows[r + parity + step][c],
                            last_dims,
                            preferred_element_type=jnp.float32,
                        )
                later_out[f, 2 * r + parity] = total.astype(later_out.dtype)

    spreads = [doubling(cols, c) for c in range(3)]
    place = lax.broadcasted_iota(jnp.int32, (2 * cols, channels), 0)
    wide_rows = []
    for cells, left, right in rim_lines(frame0, rim, spans, sizes, 0):
        wide = [doubled(m, cells.astype(jnp.bfloat16)) for m in spreads]
        wide[0] = jnp.where(place == 0, left, wide[0])
        wide[2] = jnp.where(place == 2 * cols - 1, right, wide[2])
        wide_rows.append([value.astype(jnp.bfloat16) for value in wide])
    for r in range(rows):
        for parity in range(2):
            total = bias_row[...]
            for step in range(2):
                for c in range(3):
                    total = total + lax.dot_general(
                        wide_rows[r + parity + step][c],
                        taps[parity, step, c],
                        last_dims,
                        preferred_element_type=jnp.float32,
                    )
            first_out[2 * r + parity] = total.astype(first_out.dtype)


def upsampled(summed, up_weight, up_bias):
    frames, rows, cols, channels = summed.shape
    groups = lax.axis_size("tm")
    sizes = lax.axis_size("height"), groups
    spans, _ = spans_of(1, rows, cols)
    rim, later, edge = spread(summed)
    held, outs = (frames - 1) // groups, up_weight.shape[-1]
    local = pl.BlockSpec(memory_space=pltpu.VMEM)
    first, images = pl.pallas_call(
        functools.partial(up_kernel, spans, sizes),
        out_shape=(
            jax.ShapeDtypeStruct((2 * rows, 2 * cols, outs), summed.dtype),
            jax.ShapeDtypeStruct((held, 2 * rows, outs, 2 * cols * groups), summed.dtype),
        ),
        in_specs=[local] * 7,
        out_specs=(local, local),
        compiler_params=pltpu.CompilerParams(vmem_limit_bytes=40 * 2**20),
    )(
        summed[:1],
        rim,
        later,
        edge,
        up_weight.transpose(0, 1, 3, 2),
        up_bias.reshape(1, outs),
        up_bias.reshape(outs, 1),
    )
    return first, images.transpose(0, 1, 3, 2)


def body(latents, gain_in, weight_in, bias_in, gain_mid, weight_mid, bias_mid, up_weight, up_bias):
    inner = normed_silu(latents.astype(jnp.float32), gain_in).astype(jnp.bfloat16)
    middle = conv(inner, weight_in, bias_in, gain_mid, 0, False)
    summed = conv(middle, weight_mid, bias_mid, latents, 1, True)
    return upsampled(summed, up_weight, up_bias)


def solution(mesh):
    return jax.shard_map(
        body,
        mesh=mesh,
        in_specs=(P(None, "height", "tm", None), P(), P(), P(), P(), P(), P(), P(), P()),
        out_specs=(P("height", "tm", None), P("tm", "height", None, None)),
        check_vma=False,
    )
```

profile of v0, /device:TPU:1, one launch (start us, length us, event | category | flops | bytes accessed | tf_op | source)
XLA Modules:
  0.0 84.5 jit_solution(15379655226062174037)
XLA Ops:
  0.6 0.7 reshape.114.bias
  1.3 0.7 reshape.115.other
  2.0 0.7 reshape.124.bias
  2.7 1.2 %fusion = f32[9,2,32]{2,1,0:T(2,128)S(1)} fusion(bf16[9,2,32,384]{3,2,1,0:T(8,128)(2,1)} %other.1), kind=kLoop, calls=%fused_computation.2 | loop fusion | flops 662976 | bytes 444672 | tf_op jit(solution)/shard_map/reduce_sum | solution.py:20
  3.9 0.8 copy.25.bias_col
  4.7 1.4 %fusion.6.x = bf16[9,2,32,384]{3,2,1,0:T(8,128)(2,1)S(1)} fusion(bf16[9,2,32,384]{3,2,1,0:T(8,128)(2,1)} %other.1, f32[384]{0:T(512)} %param.10, f32[9,2,32]{2,1,0:T(2,128)S(1)} %add_rsqrt_fusion), kind=kLoop, calls=%fused_computation.8 | loop fusion | flops 1548288 | bytes 888576 | tf_op jit(solution)/shard_map/convert_element_type | solution.py:416
  6.0 0.2 slice_reduce_fusion.2
  6.3 0.0 copy-start.2
  6.6 0.0 copy-start.10
  6.6 0.8 copy-done.10
  7.4 10.6 %shard_map.104.rim = bf16[704,384]{1,0:T(8,128)(2,1)} custom-call(bf16[704,384]{1,0:T(8,128)(2,1)} %copy-done.10), custom_call_target="tpu_custom_call" | custom-call | tf_op jit(solution)/shard_map/pallas_call | solution.py:102
  18.0 0.0 copy-start
  18.0 3.3 %copy-done = bf16[3,3,3,384,384]{4,3,2,1,0:T(8,128)(2,1)S(1)} copy-done((bf16[3,3,3,384,384]{4,3,2,1,0:T(8,128)(2,1)S(1)}, bf16[3,3,3,384,384]{4,3,2,1,0:T(8,128)(2,1)}, u32[]{:S(2)}) %copy-start) | copy-done | bytes 7962648
  21.3 0.0 copy-start.3
  21.3 1.0 %copy-done.3 = bf16[704,384]{1,0:T(8,128)(2,1)S(1)} copy-done((bf16[704,384]{1,0:T(8,128)(2,1)S(1)}, bf16[704,384]{1,0:T(8,128)(2,1)}, u32[]{:S(2)}) %copy-start.3) | copy-done | bytes 540696
  22.3 9.9 %shard_map.105.x = bf16[9,2,32,384]{3,2,1,0:T(8,128)(2,1)S(1)} custom-call(bf16[9,2,32,384]{3,2,1,0:T(8,128)(2,1)S(1)} %fusion.6.x, bf16[704,384]{1,0:T(8,128)(2,1)S(1)} %copy-done.3, bf16[3,3,3,384,384]{4,3,2,1,0:T(8,128)(2,1)S(1)} %copy-done, f32[1,384]{1,0:T(1,128)S(1)} %reshape.114.bias, f32[1,384]{1,0:T(1,128)S(1)} %reshape.115.other), custom_call_target="tpu_custom_call" | custom-call | tf_op jit(solution)/shard_map/pallas_call | solution.py:292
  32.3 0.0 copy-start.5
  32.3 0.0 copy-start.9
  32.3 0.2 slice_reduce_fusion
  32.9 0.0 copy-start.11
  32.9 0.8 copy-done.11
  33.7 9.8 %shard_map.106.rim = bf16[704,384]{1,0:T(8,128)(2,1)} custom-call(bf16[704,384]{1,0:T(8,128)(2,1)} %copy-done.11), custom_call_target="tpu_custom_call" | custom-call | tf_op jit(solution)/shard_map/pallas_call | solution.py:102
  43.5 0.0 copy-done.2
  43.5 0.0 copy-start.1
  43.6 3.3 %copy-done.1 = bf16[3,3,3,384,384]{4,3,2,1,0:T(8,128)(2,1)S(1)} copy-done((bf16[3,3,3,384,384]{4,3,2,1,0:T(8,128)(2,1)S(1)}, bf16[3,3,3,384,384]{4,3,2,1,0:T(8,128)(2,1)}, u32[]{:S(2)}) %copy-start.1) | copy-done | bytes 7962648
  46.8 0.0 copy-start.4
  46.8 1.0 %copy-done.4 = bf16[704,384]{1,0:T(8,128)(2,1)S(1)} copy-done((bf16[704,384]{1,0:T(8,128)(2,1)S(1)}, bf16[704,384]{1,0:T(8,128)(2,1)}, u32[]{:S(2)}) %copy-start.4) | copy-done | bytes 540696
  47.9 9.6 %shard_map.107 = bf16[9,2,32,384]{3,2,1,0:T(8,128)(2,1)S(1)} custom-call(bf16[9,2,32,384]{3,2,1,0:T(8,128)(2,1)S(1)} %shard_map.105.x, bf16[704,384]{1,0:T(8,128)(2,1)S(1)} %copy-done.4, bf16[3,3,3,384,384]{4,3,2,1,0:T(8,128)(2,1)S(1)} %copy-done.1, f32[1,384]{1,0:T(1,128)S(1)} %reshape.124.bias, bf16[9,2,32,384]{3,2,1,0:T(8,128)(2,1)S(1)} %copy-done.2), custom_call_target="tpu_custom_call" | custom-call | tf_op jit(solution)/shard_map/pallas_call | solution.py:292
  57.7 0.0 copy-start.12
  57.7 0.8 copy.24
  58.5 0.0 copy-done.12
  58.5 16.6 %shard_map.108 = (bf16[160,384]{1,0:T(8,128)(2,1)}, bf16[4,128,384]{2,1,0:T(8,128)(2,1)}, bf16[2,4,64,384]{3,2,1,0:T(8,128)(2,1)}) custom-call(bf16[160,384]{1,0:T(8,128)(2,1)} %copy-done.12, bf16[4,128,384]{2,1,0:T(8,128)(2,1)} %bitcast.58), custom_call_target="tpu_custom_call" | custom-call | tf_op jit(solution)/shard_map/pallas_call | solution.py:208
  75.1 0.0 copy-done.5
  75.1 0.0 copy-done.9
  75.1 0.0 copy-start.6
  75.1 1.0 %copy-done.6 = bf16[4,128,384]{2,1,0:T(8,128)(2,1)S(1)} copy-done((bf16[4,128,384]{2,1,0:T(8,128)(2,1)S(1)}, bf16[4,128,384]{2,1,0:T(8,128)(2,1)}, u32[]{:S(2)}) %copy-start.6) | copy-done | bytes 393240
  76.1 0.0 copy-start.7
  76.1 1.0 %copy-done.7 = bf16[2,4,64,384]{3,2,1,0:T(8,128)(2,1)S(1)} copy-done((bf16[2,4,64,384]{3,2,1,0:T(8,128)(2,1)S(1)}, bf16[2,4,64,384]{3,2,1,0:T(8,128)(2,1)}, u32[]{:S(2)}) %copy-start.7) | copy-done | bytes 393240
  77.1 0.0 copy-start.8
  77.1 0.9 %copy-done.8 = bf16[160,384]{1,0:T(8,128)(2,1)S(1)} copy-done((bf16[160,384]{1,0:T(8,128)(2,1)S(1)}, bf16[160,384]{1,0:T(8,128)(2,1)}, u32[]{:S(2)}) %copy-start.8) | copy-done | bytes 122904
  78.0 6.5 %shard_map.109 = (bf16[4,64,192]{2,1,0:T(8,128)(2,1)}, bf16[2,4,192,256]{3,2,1,0:T(8,128)(2,1)}) custom-call(bf16[1,2,32,384]{3,2,1,0:T(8,128)(2,1)S(1)} %slice.149.frame0, bf16[160,384]{1,0:T(8,128)(2,1)S(1)} %copy-done.8, bf16[4,128,384]{2,1,0:T(8,128)(2,1)S(1)} %copy-done.6, bf16[2,4,64,384]{3,2,1,0:T(8,128)(2,1)S(1)} %copy-done.7, ...), custom_call_target="tpu_custom_call" | custom-call | tf_op jit(solution)/shard_map/pallas_call | solution.py:394
  (45 shorter events, 0.8 us)
Async XLA Ops:
  6.3 37.2 %copy-start.2 = (bf16[9,2,32,384]{3,2,1,0:T(8,128)(2,1)S(1)}, bf16[9,2,32,384]{3,2,1,0:T(8,128)(2,1)}, u32[]{:S(2)}) copy-start(bf16[9,2,32,384]{3,2,1,0:T(8,128)(2,1)} %other.1) | copy-start | bytes 1327108
  6.6 0.8 copy-start.10
  18.0 3.3 %copy-start = (bf16[3,3,3,384,384]{4,3,2,1,0:T(8,128)(2,1)S(1)}, bf16[3,3,3,384,384]{4,3,2,1,0:T(8,128)(2,1)}, u32[]{:S(2)}) copy-start(bf16[3,3,3,384,384]{4,3,2,1,0:T(8,128)(2,1)} %w.2) | copy-start | bytes 23887876
  21.3 1.0 %copy-start.3 = (bf16[704,384]{1,0:T(8,128)(2,1)S(1)}, bf16[704,384]{1,0:T(8,128)(2,1)}, u32[]{:S(2)}) copy-start(bf16[704,384]{1,0:T(8,128)(2,1)} %shard_map.104.rim) | copy-start | bytes 1622020
  32.3 42.8 %copy-start.5 = (bf16[3,3,384,192]{2,3,1,0:T(8,128)(2,1)S(1)}, bf16[3,3,384,192]{2,3,1,0:T(8,128)(2,1)}, u32[]{:S(2)}) copy-start(bf16[3,3,384,192]{2,3,1,0:T(8,128)(2,1)} %param.16) | copy-start | bytes 3981316
  32.3 42.8 %copy-start.9 = (f32[192]{0:T(256)S(1)}, f32[192]{0:T(256)}, u32[]{:S(2)}) copy-start(f32[192]{0:T(256)} %param.17) | copy-start | bytes 2308
  32.9 0.8 copy-start.11
  43.5 3.3 %copy-start.1 = (bf16[3,3,3,384,384]{4,3,2,1,0:T(8,128)(2,1)S(1)}, bf16[3,3,3,384,384]{4,3,2,1,0:T(8,128)(2,1)}, u32[]{:S(2)}) copy-start(bf16[3,3,3,384,384]{4,3,2,1,0:T(8,128)(2,1)} %w.3) | copy-start | bytes 23887876
  46.8 1.0 %copy-start.4 = (bf16[704,384]{1,0:T(8,128)(2,1)S(1)}, bf16[704,384]{1,0:T(8,128)(2,1)}, u32[]{:S(2)}) copy-start(bf16[704,384]{1,0:T(8,128)(2,1)} %shard_map.106.rim) | copy-start | bytes 1622020
  57.7 0.8 copy-start.12
  75.1 1.0 %copy-start.6 = (bf16[4,128,384]{2,1,0:T(8,128)(2,1)S(1)}, bf16[4,128,384]{2,1,0:T(8,128)(2,1)}, u32[]{:S(2)}) copy-start(bf16[4,128,384]{2,1,0:T(8,128)(2,1)} %get-tuple-element.8.later) | copy-start | bytes 1179652
  76.1 1.0 %copy-start.7 = (bf16[2,4,64,384]{3,2,1,0:T(8,128)(2,1)S(1)}, bf16[2,4,64,384]{3,2,1,0:T(8,128)(2,1)}, u32[]{:S(2)}) copy-start(bf16[2,4,64,384]{3,2,1,0:T(8,128)(2,1)} %get-tuple-element.9.edge) | copy-start | bytes 1179652
  77.1 0.9 %copy-start.8 = (bf16[160,384]{1,0:T(8,128)(2,1)S(1)}, bf16[160,384]{1,0:T(8,128)(2,1)}, u32[]{:S(2)}) copy-start(bf16[160,384]{1,0:T(8,128)(2,1)} %get-tuple-element.7.rim) | copy-start | bytes 368644
where the time goes:
time: 85.1 us; the launch traced here: 84.5 us
  Pallas kernels  63.1 us (74%)
  local copies, waits for them, and re-layouts  17.9 us (21%)
  other arithmetic  2.54 us (3%)
  between operations  1.04 us (1%)
    pallas_call x2, Pallas kernels, exchanged(): pl.pallas_call(functools.partial(rim_kernel, spans, sizes), out_shape=jax...  20.5 us
    pallas_call x2, Pallas kernels, conv(): pl.pallas_call(functools.partial(conv_kernel, spans, sizes, residual), ou...  19.5 us
    pallas_call x1, Pallas kernels, spread(): pl.pallas_call(functools.partial(spread_kernel, spans, line, sizes), out_...  16.6 us
    unnamed x55, local copies, waits for them, and re-layouts  13.5 us
    pallas_call x1, Pallas kernels, upsampled(): pl.pallas_call(functools.partial(up_kernel, spans, sizes), out_shape=(jax...  6.52 us

commit v1 on v0

--- a/solution.py
+++ b/solution.py
@@ -93,20 +93,6 @@
         @pl.when(present(-dh, -dt, h, t, sizes))
         def _():
             copy(k).wait_recv()
-
-
-def exchanged(values, collective_id):
-    frames, rows, cols, channels = values.shape
-    spans, total = spans_of(frames, rows, cols)
-    sizes = lax.axis_size("height"), lax.axis_size("tm")
-    return pl.pallas_call(
-        functools.partial(rim_kernel, spans, sizes),
-        out_shape=jax.ShapeDtypeStruct((total, channels), values.dtype),
-        in_specs=[pl.BlockSpec(memory_space=pl.ANY)],
-        out_specs=pl.BlockSpec(memory_space=pl.ANY),
-        scratch_shapes=[pltpu.SemaphoreType.DMA((8,)), pltpu.SemaphoreType.DMA((8,))],
-        compiler_params=pltpu.CompilerParams(collective_id=collective_id, has_side_effects=True),
-    )(rim_pack(values))
 
 
 def spread_kernel(spans, line, sizes, first, later, first_out, later_out, edge_out, fs, fr, ls, lr, es, er, own_sem):
@@ -244,12 +230,15 @@
     return lines
 
 
-def conv_kernel(spans, sizes, residual, x, rim, w, bias, other, out, buf, acc):
+def conv_kernel(
+    spans, sizes, residual, x, packed, w, bias, other, out, buf, acc, rim, send_sems, recv_sems
+):
     frames, rows, cols, channels = x.shape
     step = pl.program_id(0)
 
     @pl.when(step == 0)
     def _():
+        rim_kernel(spans, sizes, packed, rim, send_sems, recv_sems)
         acc[...] = jnp.broadcast_to(bias[...], acc.shape)
         buf[:, 0:2] = jnp.zeros((3, 2, *buf.shape[2:]), buf.dtype)
         place = lax.broadcasted_iota(jnp.int32, (cols, channels), 0)
@@ -279,9 +268,9 @@
 
 def conv(values, weight, bias, other, collective_id, residual):
     frames, rows, cols, channels = values.shape
-    spans, _ = spans_of(frames, rows, cols)
+    spans, total = spans_of(frames, rows, cols)
     sizes = lax.axis_size("height"), lax.axis_size("tm")
-    rim = exchanged(values, collective_id)
+    packed = rim_pack(values)
     bias = bias.reshape(1, channels)
     if not residual:
         other = other.reshape(1, channels)
@@ -295,7 +284,7 @@
         grid=(9,),
         in_specs=[
             whole(values),
-            whole(rim),
+            whole(packed),
             pl.BlockSpec((1, 1, *weight.shape[2:]), lambda i: (i // 3, i % 3, 0, 0, 0)),
             whole(bias),
             whole(other),
@@ -304,9 +293,14 @@
         scratch_shapes=[
             pltpu.VMEM((3, frames + 2, rows + 2, cols, channels), values.dtype),
             pltpu.VMEM((frames * rows * cols, channels), jnp.float32),
+            pltpu.VMEM((total, channels), values.dtype),
+            pltpu.SemaphoreType.DMA((8,)),
+            pltpu.SemaphoreType.DMA((8,)),
         ],
-        compiler_params=pltpu.CompilerParams(vmem_limit_bytes=40 * 2**20),
-    )(values, rim, weight, bias, other)
+        compiler_params=pltpu.CompilerParams(
+            collective_id=collective_id, has_side_effects=True, vmem_limit_bytes=58 * 2**20
+        ),
+    )(values, packed, weight, bias, other)
 
 
 def doubling(cols, offset):

time: 85.1 us -> 89.1 us (1.047)
  Pallas kernels: 63.1 us -> 68.6 us
  local copies, waits for them, and re-layouts: 17.9 us -> 15.6 us
    pallas_call x2, Pallas kernels: 19.5 us -> 45.5 us  [conv(): pl.pallas_call(functools.partial(conv_kernel, spans, sizes, residual), ou...]
    pallas_call x2 -> x0, Pallas kernels: 20.5 us -> none  [exchanged(): pl.pallas_call(functools.partial(rim_kernel, spans, sizes), out_shape=jax...]
    unnamed x55 -> x45, local copies, waits for them, and re-layouts: 13.5 us -> 5.05 us
    slice x5 -> x6, local copies, waits for them, and re-layouts: 0.42 us -> 2.84 us  [rim_pack(): piece = piece[:, :, :1] if dt < 0 else piece[:, :, -1:]]
    slice x2 -> x4, local copies, waits for them, and re-layouts: 0.09 us -> 1.27 us  [rim_pack(): piece = piece[:, :1] if dh < 0 else piece[:, -1:]]
    slice x1, local copies, waits for them, and re-layouts: 0.04 us -> 1.08 us  [spread(): summed[1:].reshape(groups, held, rows, cols, channels)]
    convert_element_type x0 -> x1, local copies, waits for them, and re-layouts: none -> 0.94 us  [body(): normed_silu(latents.astype(jnp.float32), gain_in).astype(jnp.bfloat16)]
where the time goes in v1:
time: 89.1 us; the launch traced here: 88.1 us
  Pallas kernels  68.6 us (77%)
  local copies, waits for them, and re-layouts  15.6 us (18%)
  other arithmetic  2.99 us (3%)
  between operations  0.96 us (1%)
    pallas_call x2, Pallas kernels, conv(): pl.pallas_call(functools.partial(conv_kernel, spans, sizes, residual), ou...  45.5 us
    pallas_call x1, Pallas kernels, spread(): pl.pallas_call(functools.partial(spread_kernel, spans, line, sizes), out_...  16.6 us
    pallas_call x1, Pallas kernels, upsampled(): pl.pallas_call(functools.partial(up_kernel, spans, sizes), out_shape=(jax...  6.51 us
    unnamed x45, local copies, waits for them, and re-layouts  5.05 us
    slice x6, local copies, waits for them, and re-layouts, rim_pack(): piece = piece[:, :, :1] if dt < 0 else piece[:, :, -1:]  2.84 us

profile of v1, /device:TPU:1, one launch (start us, length us, event | category | flops | bytes accessed | tf_op | source)
XLA Modules:
  0.0 88.1 jit_solution(17514762478078896368)
XLA Ops:
  0.6 1.4 %fusion = f32[9,2,32]{0,2,1:T(8,128)S(1)} fusion(bf16[9,2,32,384]{3,2,1,0:T(8,128)(2,1)} %other.1), kind=kLoop, calls=%fused_computation.2 | loop fusion | flops 662976 | bytes 444672 | tf_op jit(solution)/shard_map/reduce_sum | solution.py:20
  2.0 1.6 %fusion.6 = bf16[9,2,32,384]{3,0,2,1:T(8,128)(2,1)S(1)} fusion(bf16[9,2,32,384]{3,2,1,0:T(8,128)(2,1)} %other.1, f32[384]{0:T(512)} %param.10, f32[9,2,32]{0,2,1:T(8,128)S(1)} %add_rsqrt_fusion), kind=kLoop, calls=%fused_computation.8 | loop fusion | flops 1548288 | bytes 888576 | tf_op jit(solution)/shard_map/convert_element_type | solution.py:410
  3.6 0.1 fusion.8
  3.8 0.0 copy-start.8
  3.8 0.0 copy-start.9
  4.2 0.0 copy-start.5
  4.2 0.9 %copy.25.x = bf16[9,2,32,384]{3,2,1,0:T(8,128)(2,1)} copy(bf16[9,2,32,384]{3,0,2,1:T(8,128)(2,1)S(1)} %fusion.6) | data formatting | bytes 884736 | tf_op jit(solution)/shard_map/convert_element_type | solution.py:410
  5.1 0.0 copy-done.8
  5.1 0.6 reshape.114.bias
  5.7 0.0 copy-done.9
  5.7 0.6 reshape.115.other
  6.3 0.0 copy-done.5
  6.3 23.2 %shard_map.104.x = bf16[9,2,32,384]{3,2,1,0:T(8,128)(2,1)} custom-call(bf16[9,2,32,384]{3,2,1,0:T(8,128)(2,1)} %copy.25.x, bf16[704,384]{1,0:T(8,128)(2,1)} %copy-done.5, bf16[3,3,3,384,384]{4,3,2,1,0:T(8,128)(2,1)} %w.2, f32[1,384]{1,0:T(1,128)} %reshape.114.bias, f32[1,384]{1,0:T(1,128)} %reshape.115.other), custom_call_target="tpu_custom_call" | custom-call | tf_op jit(solution)/shard_map/pallas_call | solution.py:281
  29.5 0.0 copy-start.10
  29.5 1.1 %fusion.11 = (bf16[9,1,32,384]{3,2,1,0:T(8,128)(2,1)S(1)}, bf16[9,1,32,384]{3,2,1,0:T(8,128)(2,1)S(1)}) fusion(bf16[9,2,32,384]{3,2,1,0:T(8,128)(2,1)} %shard_map.104.x), kind=kLoop, calls=%fused_computation.54 | loop fusion | bytes 884736 | tf_op jit(solution)/shard_map/slice | solution.py:45
  30.7 1.1 %slice_reduce_fusion = (bf16[9,2,384]{2,1,0:T(2,128)(2,1)S(1)}, bf16[9,2,384]{2,1,0:T(2,128)(2,1)S(1)}) fusion(bf16[9,2,32,384]{3,2,1,0:T(8,128)(2,1)} %shard_map.104.x), kind=kLoop, calls=%fused_computation.34 | loop fusion | bytes 55296 | tf_op jit(solution)/shard_map/slice | solution.py:47
  31.9 0.9 %fusion.10 = (bf16[9,1,1,384]{3,2,1,0:T(2,128)(2,1)S(1)}, bf16[9,1,1,384]{3,2,1,0:T(2,128)(2,1)S(1)}, bf16[9,1,1,384]{3,2,1,0:T(2,128)(2,1)S(1)}, bf16[9,1,1,384]{3,2,1,0:T(2,128)(2,1)S(1)}) fusion(bf16[9,2,32,384]{3,2,1,0:T(8,128)(2,1)} %shard_map.104.x), kind=kLoop, calls=%fused_computation.53 | loop fusion | bytes 55296 | tf_op jit(solution)/shard_map/slice | solution.py:47
  33.0 0.0 copy-done.10
  33.0 0.0 copy-start.6
  33.0 0.6 reshape.124.bias
  33.6 0.2 copy-done.6
  33.8 22.3 %shard_map.105 = bf16[9,2,32,384]{3,2,1,0:T(8,128)(2,1)} custom-call(bf16[9,2,32,384]{3,2,1,0:T(8,128)(2,1)} %shard_map.104.x, bf16[704,384]{1,0:T(8,128)(2,1)} %copy-done.6, bf16[3,3,3,384,384]{4,3,2,1,0:T(8,128)(2,1)} %w.3, f32[1,384]{1,0:T(1,128)} %reshape.124.bias, bf16[9,2,32,384]{3,2,1,0:T(8,128)(2,1)} %other.1), custom_call_target="tpu_custom_call" | custom-call | tf_op jit(solution)/shard_map/pallas_call | solution.py:281
  56.1 0.0 copy-start.4
  56.1 0.0 copy-start
  56.1 0.8 constant_dynamic-update-slice_fusion.23
  56.9 0.7 constant_dynamic-update-slice_fusion.22
  57.7 0.7 fusion.9
  58.5 0.8 slice_bitcast_fusion.4
  59.3 0.0 copy-start.7
  59.3 1.1 %slice.132 = bf16[8,2,32,384]{3,2,1,0:T(8,128)(2,1)S(1)} slice(bf16[9,2,32,384]{3,2,1,0:T(8,128)(2,1)} %shard_map.105), slice={[1:9], [0:2], [0:32], [0:384]} | slice | bytes 786432 | tf_op jit(solution)/shard_map/slice | solution.py:190
  60.4 0.8 copy.32
  61.2 0.0 copy-done.7
  61.2 16.6 %shard_map.106 = (bf16[160,384]{1,0:T(8,128)(2,1)}, bf16[4,128,384]{2,1,0:T(8,128)(2,1)}, bf16[2,4,64,384]{3,2,1,0:T(8,128)(2,1)}) custom-call(bf16[160,384]{1,0:T(8,128)(2,1)} %copy-done.7, bf16[4,128,384]{2,1,0:T(8,128)(2,1)} %bitcast.53), custom_call_target="tpu_custom_call" | custom-call | tf_op jit(solution)/shard_map/pallas_call | solution.py:194
  77.8 0.8 slice.123.frame0
  78.6 0.0 copy-done.4
  78.6 0.1 copy.33.bias_col
  78.7 0.0 copy-done
  78.7 0.0 copy-start.1
  78.7 1.0 %copy-done.1 = bf16[4,128,384]{2,1,0:T(8,128)(2,1)S(1)} copy-done((bf16[4,128,384]{2,1,0:T(8,128)(2,1)S(1)}, bf16[4,128,384]{2,1,0:T(8,128)(2,1)}, u32[]{:S(2)}) %copy-start.1) | copy-done | bytes 393240
  79.7 0.0 copy-start.2
  79.7 1.0 %copy-done.2 = bf16[2,4,64,384]{3,2,1,0:T(8,128)(2,1)S(1)} copy-done((bf16[2,4,64,384]{3,2,1,0:T(8,128)(2,1)S(1)}, bf16[2,4,64,384]{3,2,1,0:T(8,128)(2,1)}, u32[]{:S(2)}) %copy-start.2) | copy-done | bytes 393240
  80.7 0.0 copy-start.3
  80.7 0.9 %copy-done.3 = bf16[160,384]{1,0:T(8,128)(2,1)S(1)} copy-done((bf16[160,384]{1,0:T(8,128)(2,1)S(1)}, bf16[160,384]{1,0:T(8,128)(2,1)}, u32[]{:S(2)}) %copy-start.3) | copy-done | bytes 122904
  81.6 6.5 %shard_map.107 = (bf16[4,64,192]{2,1,0:T(8,128)(2,1)}, bf16[2,4,192,256]{3,2,1,0:T(8,128)(2,1)}) custom-call(bf16[1,2,32,384]{3,2,1,0:T(8,128)(2,1)S(1)} %slice.123.frame0, bf16[160,384]{1,0:T(8,128)(2,1)S(1)} %copy-done.3, bf16[4,128,384]{2,1,0:T(8,128)(2,1)S(1)} %copy-done.1, bf16[2,4,64,384]{3,2,1,0:T(8,128)(2,1)S(1)} %copy-done.2, ...), custom_call_target="tpu_custom_call" | custom-call | tf_op jit(solution)/shard_map/pallas_call | solution.py:388
  (37 shorter events, 0.7 us)
Async XLA Ops:
  3.8 1.3 %copy-start.8 = (f32[384]{0:T(512)S(1)}, f32[384]{0:T(512)}, u32[]{:S(2)}) copy-start(f32[384]{0:T(512)} %param.12) | copy-start | bytes 4612
  3.8 1.9 %copy-start.9 = (f32[384]{0:T(512)S(1)}, f32[384]{0:T(512)}, u32[]{:S(2)}) copy-start(f32[384]{0:T(512)} %param.13) | copy-start | bytes 4612
  4.2 2.1 %copy-start.5 = (bf16[704,384]{1,0:T(8,128)(2,1)}, bf16[704,384]{1,0:T(8,128)(2,1)S(1)}, u32[]{:S(2)}) copy-start(bf16[704,384]{1,0:T(8,128)(2,1)S(1)} %constant_dynamic-update-slice_fusion.packed) | copy-start | bytes 1622020
  29.5 3.5 %copy-start.10 = (f32[384]{0:T(512)S(1)}, f32[384]{0:T(512)}, u32[]{:S(2)}) copy-start(f32[384]{0:T(512)} %param.15) | copy-start | bytes 4612
  33.0 0.8 copy-start.6
  56.1 22.5 %copy-start.4 = (f32[192]{0:T(256)S(1)}, f32[192]{0:T(256)}, u32[]{:S(2)}) copy-start(f32[192]{0:T(256)} %param.17) | copy-start | bytes 2308
  56.1 22.6 %copy-start = (bf16[3,3,384,192]{2,3,1,0:T(8,128)(2,1)S(1)}, bf16[3,3,384,192]{2,3,1,0:T(8,128)(2,1)}, u32[]{:S(2)}) copy-start(bf16[3,3,384,192]{2,3,1,0:T(8,128)(2,1)} %param.16) | copy-start | bytes 3981316
  59.3 1.9 %copy-start.7 = (bf16[160,384]{1,0:T(8,128)(2,1)}, bf16[160,384]{1,0:T(8,128)(2,1)S(1)}, u32[]{:S(2)}) copy-start(bf16[160,384]{1,0:T(8,128)(2,1)S(1)} %constant_dynamic-update-slice_fusion.16.first) | copy-start | bytes 368644
  78.7 1.0 %copy-start.1 = (bf16[4,128,384]{2,1,0:T(8,128)(2,1)S(1)}, bf16[4,128,384]{2,1,0:T(8,128)(2,1)}, u32[]{:S(2)}) copy-start(bf16[4,128,384]{2,1,0:T(8,128)(2,1)} %get-tuple-element.8.later) | copy-start | bytes 1179652
  79.7 1.0 %copy-start.2 = (bf16[2,4,64,384]{3,2,1,0:T(8,128)(2,1)S(1)}, bf16[2,4,64,384]{3,2,1,0:T(8,128)(2,1)}, u32[]{:S(2)}) copy-start(bf16[2,4,64,384]{3,2,1,0:T(8,128)(2,1)} %get-tuple-element.9.edge) | copy-start | bytes 1179652
  80.7 0.9 %copy-start.3 = (bf16[160,384]{1,0:T(8,128)(2,1)S(1)}, bf16[160,384]{1,0:T(8,128)(2,1)}, u32[]{:S(2)}) copy-start(bf16[160,384]{1,0:T(8,128)(2,1)} %get-tuple-element.7.rim) | copy-start | bytes 368644

commit v2 on v1

--- a/solution.py
+++ b/solution.py
@@ -298,7 +298,7 @@
             pltpu.SemaphoreType.DMA((8,)),
         ],
         compiler_params=pltpu.CompilerParams(
-            collective_id=collective_id, has_side_effects=True, vmem_limit_bytes=58 * 2**20
+            collective_id=collective_id, has_side_effects=True, vmem_limit_bytes=53 * 2**20
         ),
     )(values, packed, weight, bias, other)
 

time: 89.1 us -> 78.1 us (0.88)
  local copies, waits for them, and re-layouts: 15.6 us -> 6.6 us
  Pallas kernels: 68.6 us -> 66.8 us
    slice x6, local copies, waits for them, and re-layouts: 2.84 us -> 0.25 us  [rim_pack(): piece = piece[:, :, :1] if dt < 0 else piece[:, :, -1:]]
    pallas_call x2, Pallas kernels: 45.5 us -> 43.7 us  [conv(): pl.pallas_call(functools.partial(conv_kernel, spans, sizes, residual), ou...]
    reshape x2, local copies, waits for them, and re-layouts: 1.17 us -> 0.01 us  [conv(): bias = bias.reshape(1, channels)]
    slice x4, local copies, waits for them, and re-layouts: 1.27 us -> 0.22 us  [rim_pack(): piece = piece[:, :1] if dh < 0 else piece[:, -1:]]
    slice x1, local copies, waits for them, and re-layouts: 1.08 us -> 0.04 us  [spread(): summed[1:].reshape(groups, held, rows, cols, channels)]
where the time goes in v2:
time: 78.1 us; the launch traced here: 77.4 us
  Pallas kernels  66.8 us (86%)
  local copies, waits for them, and re-layouts  6.6 us (8%)
  other arithmetic  2.99 us (4%)
  between operations  1.01 us (1%)
    pallas_call x2, Pallas kernels, conv(): pl.pallas_call(functools.partial(conv_kernel, spans, sizes, residual), ou...  43.7 us
    pallas_call x1, Pallas kernels, spread(): pl.pallas_call(functools.partial(spread_kernel, spans, line, sizes), out_...  16.6 us
    pallas_call x1, Pallas kernels, upsampled(): pl.pallas_call(functools.partial(up_kernel, spans, sizes), out_shape=(jax...  6.51 us
    unnamed x45, local copies, waits for them, and re-layouts  4.88 us
    convert_element_type x1, other arithmetic, body(): normed_silu(latents.astype(jnp.float32), gain_in).astype(jnp.bfloat16)  1.62 us

profile of v2, /device:TPU:1, one launch (start us, length us, event | category | flops | bytes accessed | tf_op | source)
XLA Modules:
  0.0 77.4 jit_solution(16925079520586423466)
XLA Ops:
  0.6 1.4 %fusion = f32[9,2,32]{0,2,1:T(8,128)S(1)} fusion(bf16[9,2,32,384]{3,2,1,0:T(8,128)(2,1)} %other.1), kind=kLoop, calls=%fused_computation.2 | loop fusion | flops 662976 | bytes 444672 | tf_op jit(solution)/shard_map/reduce_sum | solution.py:20
  2.0 1.6 %fusion.6 = bf16[9,2,32,384]{3,0,2,1:T(8,128)(2,1)S(1)} fusion(bf16[9,2,32,384]{3,2,1,0:T(8,128)(2,1)} %other.1, f32[384]{0:T(512)} %param.10, f32[9,2,32]{0,2,1:T(8,128)S(1)} %add_rsqrt_fusion), kind=kLoop, calls=%fused_computation.8 | loop fusion | flops 1548288 | bytes 888576 | tf_op jit(solution)/shard_map/convert_element_type | solution.py:410
  3.6 0.1 fusion.8
  3.8 0.0 copy-start.8
  3.8 0.0 copy-start.9
  4.2 0.0 copy-start.5
  4.2 0.1 copy.25.x
  4.3 0.2 copy-done.8
  4.5 0.0 copy-done.9
  4.5 0.5 copy-done.5
  5.0 22.3 %shard_map.104.x = bf16[9,2,32,384]{3,2,1,0:T(8,128)(2,1)S(1)} custom-call(bf16[9,2,32,384]{3,2,1,0:T(8,128)(2,1)S(1)} %copy.25.x, bf16[704,384]{1,0:T(8,128)(2,1)} %copy-done.5, bf16[3,3,3,384,384]{4,3,2,1,0:T(8,128)(2,1)} %w.2, f32[1,384]{1,0:T(1,128)S(1)} %reshape.114.bias, f32[1,384]{1,0:T(1,128)S(1)} %reshape.115.other), custom_call_target="tpu_custom_call" | custom-call | tf_op jit(solution)/shard_map/pallas_call | solution.py:281
  27.3 0.0 copy-start.10
  27.5 0.2 slice_reduce_fusion
  27.9 0.1 copy-done.10
  28.0 0.0 copy-start.6
  28.0 0.8 %copy-done.6 = bf16[704,384]{1,0:T(8,128)(2,1)} copy-done((bf16[704,384]{1,0:T(8,128)(2,1)}, bf16[704,384]{1,0:T(8,128)(2,1)S(1)}, u32[]{:S(2)}) %copy-start.6) | copy-done | bytes 540696
  28.8 21.3 %shard_map.105 = bf16[9,2,32,384]{3,2,1,0:T(8,128)(2,1)S(1)} custom-call(bf16[9,2,32,384]{3,2,1,0:T(8,128)(2,1)S(1)} %shard_map.104.x, bf16[704,384]{1,0:T(8,128)(2,1)} %copy-done.6, bf16[3,3,3,384,384]{4,3,2,1,0:T(8,128)(2,1)} %w.3, f32[1,384]{1,0:T(1,128)S(1)} %reshape.124.bias, bf16[9,2,32,384]{3,2,1,0:T(8,128)(2,1)} %other.1), custom_call_target="tpu_custom_call" | custom-call | tf_op jit(solution)/shard_map/pallas_call | solution.py:281
  50.2 0.0 copy-start.4
  50.2 0.0 copy-start
  50.4 0.0 copy-start.7
  50.4 0.8 %copy.32 = bf16[4,2,2,32,384]{4,3,1,2,0:T(8,128)(2,1)} copy(bf16[4,2,2,32,384]{4,3,2,1,0:T(8,128)(2,1)S(1)} %bitcast.54) | data formatting | bytes 786432 | tf_op jit(solution)/shard_map/reshape | solution.py:190
  51.2 0.0 copy-done.7
  51.2 16.6 %shard_map.106 = (bf16[160,384]{1,0:T(8,128)(2,1)}, bf16[4,128,384]{2,1,0:T(8,128)(2,1)}, bf16[2,4,64,384]{3,2,1,0:T(8,128)(2,1)}) custom-call(bf16[160,384]{1,0:T(8,128)(2,1)} %copy-done.7, bf16[4,128,384]{2,1,0:T(8,128)(2,1)} %bitcast.53), custom_call_target="tpu_custom_call" | custom-call | tf_op jit(solution)/shard_map/pallas_call | solution.py:194
  67.8 0.0 copy-done.4
  67.8 0.1 copy.33.bias_col
  68.0 0.0 copy-done
  68.0 0.0 copy-start.1
  68.0 1.0 %copy-done.1 = bf16[4,128,384]{2,1,0:T(8,128)(2,1)S(1)} copy-done((bf16[4,128,384]{2,1,0:T(8,128)(2,1)S(1)}, bf16[4,128,384]{2,1,0:T(8,128)(2,1)}, u32[]{:S(2)}) %copy-start.1) | copy-done | bytes 393240
  69.0 0.0 copy-start.2
  69.0 1.0 %copy-done.2 = bf16[2,4,64,384]{3,2,1,0:T(8,128)(2,1)S(1)} copy-done((bf16[2,4,64,384]{3,2,1,0:T(8,128)(2,1)S(1)}, bf16[2,4,64,384]{3,2,1,0:T(8,128)(2,1)}, u32[]{:S(2)}) %copy-start.2) | copy-done | bytes 393240
  70.0 0.0 copy-start.3
  70.0 0.9 %copy-done.3 = bf16[160,384]{1,0:T(8,128)(2,1)S(1)} copy-done((bf16[160,384]{1,0:T(8,128)(2,1)S(1)}, bf16[160,384]{1,0:T(8,128)(2,1)}, u32[]{:S(2)}) %copy-start.3) | copy-done | bytes 122904
  70.9 6.5 %shard_map.107 = (bf16[4,64,192]{2,1,0:T(8,128)(2,1)}, bf16[2,4,192,256]{3,2,1,0:T(8,128)(2,1)}) custom-call(bf16[1,2,32,384]{3,2,1,0:T(8,128)(2,1)S(1)} %slice.123.frame0, bf16[160,384]{1,0:T(8,128)(2,1)S(1)} %copy-done.3, bf16[4,128,384]{2,1,0:T(8,128)(2,1)S(1)} %copy-done.1, bf16[2,4,64,384]{3,2,1,0:T(8,128)(2,1)S(1)} %copy-done.2, ...), custom_call_target="tpu_custom_call" | custom-call | tf_op jit(solution)/shard_map/pallas_call | solution.py:388
  (48 shorter events, 0.9 us)
Async XLA Ops:
  3.8 0.7 copy-start.8
  3.8 0.7 copy-start.9
  4.2 0.8 %copy-start.5 = (bf16[704,384]{1,0:T(8,128)(2,1)}, bf16[704,384]{1,0:T(8,128)(2,1)S(1)}, u32[]{:S(2)}) copy-start(bf16[704,384]{1,0:T(8,128)(2,1)S(1)} %constant_dynamic-update-slice_fusion.packed) | copy-start | bytes 1622020
  27.3 0.7 copy-start.10
  28.0 0.8 %copy-start.6 = (bf16[704,384]{1,0:T(8,128)(2,1)}, bf16[704,384]{1,0:T(8,128)(2,1)S(1)}, u32[]{:S(2)}) copy-start(bf16[704,384]{1,0:T(8,128)(2,1)S(1)} %constant_dynamic-update-slice_fusion.8.packed) | copy-start | bytes 1622020
  50.2 17.7 %copy-start.4 = (f32[192]{0:T(256)S(1)}, f32[192]{0:T(256)}, u32[]{:S(2)}) copy-start(f32[192]{0:T(256)} %param.17) | copy-start | bytes 2308
  50.2 17.8 %copy-start = (bf16[3,3,384,192]{2,3,1,0:T(8,128)(2,1)S(1)}, bf16[3,3,384,192]{2,3,1,0:T(8,128)(2,1)}, u32[]{:S(2)}) copy-start(bf16[3,3,384,192]{2,3,1,0:T(8,128)(2,1)} %param.16) | copy-start | bytes 3981316
  50.4 0.9 %copy-start.7 = (bf16[160,384]{1,0:T(8,128)(2,1)}, bf16[160,384]{1,0:T(8,128)(2,1)S(1)}, u32[]{:S(2)}) copy-start(bf16[160,384]{1,0:T(8,128)(2,1)S(1)} %constant_dynamic-update-slice_fusion.16.first) | copy-start | bytes 368644
  68.0 1.0 %copy-start.1 = (bf16[4,128,384]{2,1,0:T(8,128)(2,1)S(1)}, bf16[4,128,384]{2,1,0:T(8,128)(2,1)}, u32[]{:S(2)}) copy-start(bf16[4,128,384]{2,1,0:T(8,128)(2,1)} %get-tuple-element.8.later) | copy-start | bytes 1179652
  69.0 1.0 %copy-start.2 = (bf16[2,4,64,384]{3,2,1,0:T(8,128)(2,1)S(1)}, bf16[2,4,64,384]{3,2,1,0:T(8,128)(2,1)}, u32[]{:S(2)}) copy-start(bf16[2,4,64,384]{3,2,1,0:T(8,128)(2,1)} %get-tuple-element.9.edge) | copy-start | bytes 1179652
  70.0 0.9 %copy-start.3 = (bf16[160,384]{1,0:T(8,128)(2,1)S(1)}, bf16[160,384]{1,0:T(8,128)(2,1)}, u32[]{:S(2)}) copy-start(bf16[160,384]{1,0:T(8,128)(2,1)} %get-tuple-element.7.rim) | copy-start | bytes 368644

commit v3 on v2

--- a/solution.py
+++ b/solution.py
@@ -189,7 +189,7 @@
     line = held * cols
     later = summed[1:].reshape(groups, held, rows, cols, channels).transpose(0, 2, 1, 3, 4)
     later = later.reshape(groups, rows * line, channels)
-    anywhere = pl.BlockSpec(memory_space=pl.ANY)
+    anywhere = pl.BlockSpec(memory_space=pltpu.VMEM)
     dma = pltpu.SemaphoreType.DMA
     return pl.pallas_call(
         functools.partial(spread_kernel, spans, line, sizes),

time: 78.1 us -> 79.5 us (1.018)
  Pallas kernels: 66.8 us -> 68.1 us
    pallas_call x1, Pallas kernels: 16.6 us -> 18 us  [spread(): pl.pallas_call(functools.partial(spread_kernel, spans, line, sizes), out_...]
where the time goes in v3:
time: 79.5 us; the launch traced here: 78.7 us
  Pallas kernels  68.1 us (86%)
  local copies, waits for them, and re-layouts  6.6 us (8%)
  other arithmetic  2.99 us (4%)
  between operations  1.01 us (1%)
    pallas_call x2, Pallas kernels, conv(): pl.pallas_call(functools.partial(conv_kernel, spans, sizes, residual), ou...  43.7 us
    pallas_call x1, Pallas kernels, spread(): pl.pallas_call(functools.partial(spread_kernel, spans, line, sizes), out_...  18 us
    pallas_call x1, Pallas kernels, upsampled(): pl.pallas_call(functools.partial(up_kernel, spans, sizes), out_shape=(jax...  6.51 us
    unnamed x45, local copies, waits for them, and re-layouts  4.88 us
    convert_element_type x1, other arithmetic, body(): normed_silu(latents.astype(jnp.float32), gain_in).astype(jnp.bfloat16)  1.62 us

profile of v3, /device:TPU:1, one launch (start us, length us, event | category | flops | bytes accessed | tf_op | source)
XLA Modules:
  0.0 78.7 jit_solution(3550914468261707697)
XLA Ops:
  0.6 1.4 %fusion = f32[9,2,32]{0,2,1:T(8,128)S(1)} fusion(bf16[9,2,32,384]{3,2,1,0:T(8,128)(2,1)} %other.1), kind=kLoop, calls=%fused_computation.2 | loop fusion | flops 662976 | bytes 444672 | tf_op jit(solution)/shard_map/reduce_sum | solution.py:20
  2.0 1.6 %fusion.6 = bf16[9,2,32,384]{3,0,2,1:T(8,128)(2,1)S(1)} fusion(bf16[9,2,32,384]{3,2,1,0:T(8,128)(2,1)} %other.1, f32[384]{0:T(512)} %param.10, f32[9,2,32]{0,2,1:T(8,128)S(1)} %add_rsqrt_fusion), kind=kLoop, calls=%fused_computation.8 | loop fusion | flops 1548288 | bytes 888576 | tf_op jit(solution)/shard_map/convert_element_type | solution.py:410
  3.6 0.1 fusion.8
  3.8 0.0 copy-start.8
  3.8 0.0 copy-start.9
  4.2 0.0 copy-start.5
  4.2 0.1 copy.25.x
  4.3 0.2 copy-done.8
  4.5 0.0 copy-done.9
  4.5 0.5 copy-done.5
  5.0 22.3 %shard_map.104.x = bf16[9,2,32,384]{3,2,1,0:T(8,128)(2,1)S(1)} custom-call(bf16[9,2,32,384]{3,2,1,0:T(8,128)(2,1)S(1)} %copy.25.x, bf16[704,384]{1,0:T(8,128)(2,1)} %copy-done.5, bf16[3,3,3,384,384]{4,3,2,1,0:T(8,128)(2,1)} %w.2, f32[1,384]{1,0:T(1,128)S(1)} %reshape.114.bias, f32[1,384]{1,0:T(1,128)S(1)} %reshape.115.other), custom_call_target="tpu_custom_call" | custom-call | tf_op jit(solution)/shard_map/pallas_call | solution.py:281
  27.3 0.0 copy-start.10
  27.5 0.2 slice_reduce_fusion
  27.9 0.1 copy-done.10
  28.0 0.0 copy-start.6
  28.0 0.8 %copy-done.6 = bf16[704,384]{1,0:T(8,128)(2,1)} copy-done((bf16[704,384]{1,0:T(8,128)(2,1)}, bf16[704,384]{1,0:T(8,128)(2,1)S(1)}, u32[]{:S(2)}) %copy-start.6) | copy-done | bytes 540696
  28.8 21.3 %shard_map.105 = bf16[9,2,32,384]{3,2,1,0:T(8,128)(2,1)S(1)} custom-call(bf16[9,2,32,384]{3,2,1,0:T(8,128)(2,1)S(1)} %shard_map.104.x, bf16[704,384]{1,0:T(8,128)(2,1)} %copy-done.6, bf16[3,3,3,384,384]{4,3,2,1,0:T(8,128)(2,1)} %w.3, f32[1,384]{1,0:T(1,128)S(1)} %reshape.124.bias, bf16[9,2,32,384]{3,2,1,0:T(8,128)(2,1)} %other.1), custom_call_target="tpu_custom_call" | custom-call | tf_op jit(solution)/shard_map/pallas_call | solution.py:281
  50.2 0.0 copy-start.4
  50.2 0.0 copy-start
  50.4 0.0 copy-start.7
  50.4 0.8 %copy.32 = bf16[4,2,2,32,384]{4,3,1,2,0:T(8,128)(2,1)} copy(bf16[4,2,2,32,384]{4,3,2,1,0:T(8,128)(2,1)S(1)} %bitcast.54) | data formatting | bytes 786432 | tf_op jit(solution)/shard_map/reshape | solution.py:190
  51.2 0.0 copy-done.7
  51.2 18.0 %shard_map.106 = (bf16[160,384]{1,0:T(8,128)(2,1)}, bf16[4,128,384]{2,1,0:T(8,128)(2,1)}, bf16[2,4,64,384]{3,2,1,0:T(8,128)(2,1)}) custom-call(bf16[160,384]{1,0:T(8,128)(2,1)} %copy-done.7, bf16[4,128,384]{2,1,0:T(8,128)(2,1)} %bitcast.53), custom_call_target="tpu_custom_call" | custom-call | tf_op jit(solution)/shard_map/pallas_call | solution.py:194
  69.2 0.0 copy-done.4
  69.2 0.1 copy.33.bias_col
  69.3 0.0 copy-done
  69.3 0.0 copy-start.1
  69.3 1.0 %copy-done.1 = bf16[4,128,384]{2,1,0:T(8,128)(2,1)S(1)} copy-done((bf16[4,128,384]{2,1,0:T(8,128)(2,1)S(1)}, bf16[4,128,384]{2,1,0:T(8,128)(2,1)}, u32[]{:S(2)}) %copy-start.1) | copy-done | bytes 393240
  70.3 0.0 copy-start.2
  70.3 1.0 %copy-done.2 = bf16[2,4,64,384]{3,2,1,0:T(8,128)(2,1)S(1)} copy-done((bf16[2,4,64,384]{3,2,1,0:T(8,128)(2,1)S(1)}, bf16[2,4,64,384]{3,2,1,0:T(8,128)(2,1)}, u32[]{:S(2)}) %copy-start.2) | copy-done | bytes 393240
  71.3 0.0 copy-start.3
  71.3 0.9 %copy-done.3 = bf16[160,384]{1,0:T(8,128)(2,1)S(1)} copy-done((bf16[160,384]{1,0:T(8,128)(2,1)S(1)}, bf16[160,384]{1,0:T(8,128)(2,1)}, u32[]{:S(2)}) %copy-start.3) | copy-done | bytes 122904
  72.2 6.5 %shard_map.107 = (bf16[4,64,192]{2,1,0:T(8,128)(2,1)}, bf16[2,4,192,256]{3,2,1,0:T(8,128)(2,1)}) custom-call(bf16[1,2,32,384]{3,2,1,0:T(8,128)(2,1)S(1)} %slice.123.frame0, bf16[160,384]{1,0:T(8,128)(2,1)S(1)} %copy-done.3, bf16[4,128,384]{2,1,0:T(8,128)(2,1)S(1)} %copy-done.1, bf16[2,4,64,384]{3,2,1,0:T(8,128)(2,1)S(1)} %copy-done.2, ...), custom_call_target="tpu_custom_call" | custom-call | tf_op jit(solution)/shard_map/pallas_call | solution.py:388
  (48 shorter events, 0.8 us)
Async XLA Ops:
  3.8 0.7 copy-start.8
  3.8 0.7 copy-start.9
  4.2 0.8 %copy-start.5 = (bf16[704,384]{1,0:T(8,128)(2,1)}, bf16[704,384]{1,0:T(8,128)(2,1)S(1)}, u32[]{:S(2)}) copy-start(bf16[704,384]{1,0:T(8,128)(2,1)S(1)} %constant_dynamic-update-slice_fusion.packed) | copy-start | bytes 1622020
  27.3 0.7 copy-start.10
  28.0 0.8 %copy-start.6 = (bf16[704,384]{1,0:T(8,128)(2,1)}, bf16[704,384]{1,0:T(8,128)(2,1)S(1)}, u32[]{:S(2)}) copy-start(bf16[704,384]{1,0:T(8,128)(2,1)S(1)} %constant_dynamic-update-slice_fusion.8.packed) | copy-start | bytes 1622020
  50.2 19.0 %copy-start.4 = (f32[192]{0:T(256)S(1)}, f32[192]{0:T(256)}, u32[]{:S(2)}) copy-start(f32[192]{0:T(256)} %param.17) | copy-start | bytes 2308
  50.2 19.2 %copy-start = (bf16[3,3,384,192]{2,3,1,0:T(8,128)(2,1)S(1)}, bf16[3,3,384,192]{2,3,1,0:T(8,128)(2,1)}, u32[]{:S(2)}) copy-start(bf16[3,3,384,192]{2,3,1,0:T(8,128)(2,1)} %param.16) | copy-start | bytes 3981316
  50.4 0.9 %copy-start.7 = (bf16[160,384]{1,0:T(8,128)(2,1)}, bf16[160,384]{1,0:T(8,128)(2,1)S(1)}, u32[]{:S(2)}) copy-start(bf16[160,384]{1,0:T(8,128)(2,1)S(1)} %constant_dynamic-update-slice_fusion.16.first) | copy-start | bytes 368644
  69.3 1.0 %copy-start.1 = (bf16[4,128,384]{2,1,0:T(8,128)(2,1)S(1)}, bf16[4,128,384]{2,1,0:T(8,128)(2,1)}, u32[]{:S(2)}) copy-start(bf16[4,128,384]{2,1,0:T(8,128)(2,1)} %get-tuple-element.8.later) | copy-start | bytes 1179652
  70.3 1.0 %copy-start.2 = (bf16[2,4,64,384]{3,2,1,0:T(8,128)(2,1)S(1)}, bf16[2,4,64,384]{3,2,1,0:T(8,128)(2,1)}, u32[]{:S(2)}) copy-start(bf16[2,4,64,384]{3,2,1,0:T(8,128)(2,1)} %get-tuple-element.9.edge) | copy-start | bytes 1179652
  71.3 0.9 %copy-start.3 = (bf16[160,384]{1,0:T(8,128)(2,1)S(1)}, bf16[160,384]{1,0:T(8,128)(2,1)}, u32[]{:S(2)}) copy-start(bf16[160,384]{1,0:T(8,128)(2,1)} %get-tuple-element.7.rim) | copy-start | bytes 368644
